TPU v7x, 32 devices: a whole 2x2x4 slice. The times are simulated.
32 devices in a mesh: parts: 2 (over y), gx: 4 (over z), gy: 2 (over x), gz: 2 (over core).
Axes of the slice: x: 2, y: 2, z: 4, core: 2. Of those that a mesh axis runs over, the one named last changes fastest.
Arguments:
- volume: bfloat16 [56, 14, 56, 48], P(('parts', 'gx'), 'gy', 'gz'), parts along dimension 0, may hold values from -6 to 6
- w_qkv: bfloat16 [2, 48, 144], replicated, may hold values from -3 to 3
- w_proj: bfloat16 [2, 48, 48], replicated, may hold values from -0.875 to 0.875
- w_up: bfloat16 [2, 48, 192], replicated, may hold values from -0.875 to 0.875
- w_down: bfloat16 [2, 192, 48], replicated, may hold values from -0.4375 to 0.4375
- norm_gain: float32 [2, 2, 48], replicated, may hold values from 0.25 to 1.75
- conv_weight: bfloat16 [27, 48, 48], replicated, may hold values from -0.15625 to 0.15625
- conv_gain: float32 [48], replicated, may hold values from 0.25 to 1.75
Outputs:
- features: bfloat16 [56, 14, 56, 48], P(('parts', 'gx'), 'gy', 'gz'), parts along dimension 0
There are 2 independent parts, one for each index of `parts`. A program takes and returns all parts, laid end to end along the dimension named above; an argument that names none is the same for every part. Nothing has to cross between parts.
All inputs are finite; a program needn't handle non-finite values.
Results may differ from a plain program's by a relative error of at most 0.039.
The roundings to bfloat16 on the way count: a program that leaves them out, or rounds other values in their place, can miss the bound.
Values may be sent and summed in bfloat16 or wider, within the bound.
A program may use at most 64 MiB of HBM per device.

v0:
```python
import jax
import jax.numpy as jnp
from jax import lax
from jax.sharding import PartitionSpec as P

HEADS = 3
WINDOW = 7
SHIFT = 3


def shifted(value, axis, steps):
    count = lax.axis_size(axis)
    pairs = [(source, (source + steps) % count) for source in range(count)]
    return lax.ppermute(value, axis, pairs)


def layer_norm(values, gain):
    values = values.astype(jnp.float32)
    mean = jnp.mean(values, -1, keepdims=True)
    centred = values - mean
    spread = jnp.mean(centred * centred, -1, keepdims=True)
    return centred * lax.rsqrt(spread + 1e-05) * gain


def to_windows(values):
    sx, sy, sz = (values.shape[0], values.shape[1], values.shape[2])
    rest = values.shape[3:]
    shaped = values.reshape(
        (sx // WINDOW, WINDOW, sy // WINDOW, WINDOW, sz // WINDOW, WINDOW) + rest
    )
    order = (0, 2, 4, 1, 3, 5) + tuple(range(6, 6 + len(rest)))
    return jnp.transpose(shaped, order).reshape((-1, WINDOW**3) + rest)


def from_windows(values, sx, sy, sz):
    width = values.shape[-1]
    shaped = values.reshape(sx // WINDOW, sy // WINDOW, sz // WINDOW, WINDOW, WINDOW, WINDOW, width)
    return jnp.transpose(shaped, (0, 3, 1, 4, 2, 5, 6)).reshape(sx, sy, sz, width)


def attend_group(items):
    qkv, labels = items
    group, count, triple = qkv.shape
    width = triple // 3
    query = qkv[..., :width].reshape(group, count, HEADS, -1)
    keys = qkv[..., width : 2 * width].reshape(group, count, HEADS, -1)
    vals = qkv[..., 2 * width :].reshape(group, count, HEADS, -1)
    scores = jnp.einsum("gqhd,gkhd->ghqk", query, keys, preferred_element_type=jnp.float32) * (
        width // HEADS
    ) ** (-0.5)
    same = labels[:, None, :, None] == labels[:, None, None, :]
    scores = jnp.where(same, scores, -1e30)
    scores = scores - jnp.max(scores, -1, keepdims=True)
    weights = jnp.exp(scores)
    probs = (weights / jnp.sum(weights, -1, keepdims=True)).astype(jnp.bfloat16)
    mixed = jnp.einsum("ghqk,gkhd->gqhd", probs, vals, preferred_element_type=jnp.float32)
    return mixed.reshape(group, count, width).astype(jnp.bfloat16)


def attend(qkv, labels):
    total = qkv.shape[0]
    group = 4
    result = lax.map(
        attend_group,
        (
            qkv.reshape((total // group, group) + qkv.shape[1:]),
            labels.reshape(total // group, group, -1),
        ),
    )
    return result.reshape(total, WINDOW**3, -1)


def block(state, labels, w_qkv, w_proj, w_up, w_down, gains):
    sx, sy, sz, width = state.shape
    normed = layer_norm(state, gains[0]).astype(jnp.bfloat16).reshape(-1, width)
    qkv = jnp.dot(normed, w_qkv, preferred_element_type=jnp.float32).astype(jnp.bfloat16)
    qkv = qkv.reshape(sx, sy, sz, 3 * width)
    mixed = from_windows(attend(to_windows(qkv), to_windows(labels)), sx, sy, sz).reshape(-1, width)
    flat = state.reshape(-1, width).astype(jnp.float32)
    flat = (flat + jnp.dot(mixed, w_proj, preferred_element_type=jnp.float32)).astype(jnp.bfloat16)
    normed = layer_norm(flat, gains[1]).astype(jnp.bfloat16)
    upper = jax.nn.gelu(jnp.dot(normed, w_up, preferred_element_type=jnp.float32)).astype(
        jnp.bfloat16
    )
    flat = (
        flat.astype(jnp.float32) + jnp.dot(upper, w_down, preferred_element_type=jnp.float32)
    ).astype(jnp.bfloat16)
    return flat.reshape(sx, sy, sz, width)


def region(coords, length):
    return jnp.where(coords < length - WINDOW, 0, jnp.where(coords < length - SHIFT, 1, 2)).astype(
        jnp.int32
    )


def make_labels(offsets, local, whole):
    lx = region(offsets[0] + jnp.arange(local[0], dtype=jnp.int32), whole[0])
    ly = region(offsets[1] + jnp.arange(local[1], dtype=jnp.int32), whole[1])
    lz = region(offsets[2] + jnp.arange(local[2], dtype=jnp.int32), whole[2])
    return 9 * lx[:, None, None] + 3 * ly[None, :, None] + lz[None, None, :]


def conv_out(centre, padded, conv_weight, conv_gain):
    sx, sy, sz, width = centre.shape
    total = jnp.zeros((sx * sy * sz, width), jnp.float32)
    for tap in range(27):
        dx, dy, dz = (tap // 9, tap // 3 % 3, tap % 3)
        piece = padded[dx : dx + sx, dy : dy + sy, dz : dz + sz].reshape(-1, width)
        total = total + jnp.dot(piece, conv_weight[tap], preferred_element_type=jnp.float32)
    active = jax.nn.leaky_relu(layer_norm(total, conv_gain), 0.01)
    return (
        (centre.reshape(-1, width).astype(jnp.float32) + active)
        .astype(jnp.bfloat16)
        .reshape(sx, sy, sz, width)
    )


def edge_keep(length, index, count):
    places = jnp.arange(length + 2, dtype=jnp.int32)
    low = (places == 0) & (index == 0)
    high = (places == length + 1) & (index == count - 1)
    return jnp.where(low | high, 0.0, 1.0).astype(jnp.bfloat16)


def body(volume, w_qkv, w_proj, w_up, w_down, norm_gain, conv_weight, conv_gain):
    sx, sy, sz, width = volume.shape
    plain = jnp.zeros((sx, sy, sz), jnp.int32)
    state = block(volume, plain, w_qkv[0], w_proj[0], w_up[0], w_down[0], norm_gain[0])
    slab = shifted(state[:SHIFT], "gx", -1)
    state = jnp.concatenate([state[SHIFT:], slab], 0)
    slab = shifted(state[:, :SHIFT], "gy", -1)
    state = jnp.concatenate([state[:, SHIFT:], slab], 1)
    slab = shifted(state[:, :, :SHIFT], "gz", -1)
    state = jnp.concatenate([state[:, :, SHIFT:], slab], 2)
    index_x, index_y, index_z = (lax.axis_index("gx"), lax.axis_index("gy"), lax.axis_index("gz"))
    count_x, count_y, count_z = (lax.axis_size("gx"), lax.axis_size("gy"), lax.axis_size("gz"))
    labels = make_labels(
        (index_x * sx, index_y * sy, index_z * sz),
        (sx, sy, sz),
        (sx * count_x, sy * count_y, sz * count_z),
    )
    state = block(state, labels, w_qkv[1], w_proj[1], w_up[1], w_down[1], norm_gain[1])
    depth = SHIFT + 1
    slab = shifted(state[-depth:], "gx", 1)
    extended = jnp.concatenate([slab, state], 0)
    slab = shifted(extended[:, -depth:], "gy", 1)
    extended = jnp.concatenate([slab, extended], 1)
    slab = shifted(extended[:, :, -depth:], "gz", 1)
    extended = jnp.concatenate([slab, extended], 2)
    padded = extended[: sx + 2, : sy + 2, : sz + 2]
    keep = edge_keep(sx, index_x, count_x)[:, None, None, None]
    keep = keep * edge_keep(sy, index_y, count_y)[None, :, None, None]
    keep = keep * edge_keep(sz, index_z, count_z)[None, None, :, None]
    padded = padded * keep
    state = padded[1:-1, 1:-1, 1:-1]
    return conv_out(state, padded, conv_weight, conv_gain)


def solution(mesh):
    placed = (P(("parts", "gx"), "gy", "gz", None), P(), P(), P(), P(), P(), P(), P())
    return jax.shard_map(
        body,
        mesh=mesh,
        in_specs=placed,
        out_specs=P(("parts", "gx"), "gy", "gz", None),
        check_vma=False,
    )
```

profile of v0, /device:TPU:0, one launch (start us, length us, event | category | flops | bytes accessed | tf_op | source)
XLA Modules:
  0.0 122.0 jit_solution(15967346096348520852)
XLA Ops:
  0.0 1.3 %convert_reduce_fusion.1 = f32[7,7,28]{2,1,0:T(8,128)S(1)} fusion(bf16[7,7,28,48]{3,2,1,0:T(8,128)(2,1)} %param.8), kind=kLoop, calls=%fused_computation.85 | loop fusion | flops 130340 | bytes 137200 | tf_op jit(solution)/shard_map/reduce_sum | solution.py:19
  1.4 1.1 reshape.496
  6.3 4.8 %fusion.169 = (f32[4,3,343]{2,1,0:T(4,128)S(1)}, f32[4,3,343,343]{2,3,1,0:T(8,128)}) fusion(bf16[4,343,3,16]{1,3,2,0:T(8,128)(2,1)S(1)} %bitcast.193, bf16[4,343,3,16]{1,3,2,0:T(8,128)(2,1)S(1)} %bitcast.196), kind=kOutput, calls=%fused_computation.243 | convolution fusion | flops 49412924 | bytes 5927040 | tf_op jit(solution)/shard_map/while/body/eval_jaxpr/sub | solution.py:53
  11.1 3.4 %fusion.18 = bf16[4,343,3,16]{1,3,2,0:T(8,128)(2,1)S(1)} fusion(bf16[4,343,3,16]{1,3,2,0:T(8,128)(2,1)S(1)} %bitcast.197, f32[4,3,343,343]{2,3,1,0:T(8,128)} %get-tuple-element.66, f32[4,3,343]{2,1,0:T(4,128)S(1)} %get-tuple-element.65), kind=kOutput, calls=%fused_computation.55 | convolution fusion | flops 48066648 | bytes 5927040 | tf_op jit(solution)/shard_map/while/body/eval_jaxpr/ghqk,gkhd->gqhd/dot_general | solution.py:56
  14.5 1.2 copy.19
  15.7 0.7 convert_element_type.157
  17.5 0.7 fusion.14
  18.5 5.3 %collective-permute-start = (bf16[3,7,28,48]{3,2,1,0:T(8,128)(2,1)S(1)}, bf16[3,7,28,48]{3,2,1,0:T(8,128)(2,1)S(1)}, u32[]{:S(2)}, u32[]{:S(2)}) collective-permute-start(bf16[3,7,28,48]{3,2,1,0:T(8,128)(2,1)S(1)} %slice.284), channel_id=1, source_target_pairs={{0,12},{4,0},{8,4},{12,8},{1,13},{5,1},{9,5},{13,9},{2,14},{6,2},{... | collective-permute-start | bytes 169352 | tf_op jit(solution)/shard_map/ppermute | solution.py:14
  24.5 3.0 %collective-permute-done = bf16[3,7,28,48]{3,2,1,0:T(8,128)(2,1)S(1)} collective-permute-done((bf16[3,7,28,48]{3,2,1,0:T(8,128)(2,1)S(1)}, bf16[3,7,28,48]{3,2,1,0:T(8,128)(2,1)S(1)}, u32[]{:S(2)}, u32[]{:S(2)}) %collective-permute-start) | collective-permute-done | bytes 56480 | tf_op jit(solution)/shard_map/ppermute | solution.py:14
  27.5 1.5 %collective-permute-start.1 = (bf16[7,3,28,48]{3,2,1,0:T(8,128)(2,1)S(1)}, bf16[7,3,28,48]{3,2,1,0:T(8,128)(2,1)S(1)}, u32[]{:S(2)}, u32[]{:S(2)}) collective-permute-start(bf16[7,3,28,48]{3,2,1,0:T(8,128)(2,1)S(1)} %slice.363), channel_id=1, source_target_pairs={{0,2},{2,0},{1,3},{3,1},{4,6},{6,4},{5,7},{7,5},{8,10},{10,8},{9,1... | collective-permute-start | bytes 169352 | tf_op jit(solution)/shard_map/ppermute | solution.py:14
  29.4 3.5 %collective-permute-done.1 = bf16[7,3,28,48]{3,2,1,0:T(8,128)(2,1)S(1)} collective-permute-done((bf16[7,3,28,48]{3,2,1,0:T(8,128)(2,1)S(1)}, bf16[7,3,28,48]{3,2,1,0:T(8,128)(2,1)S(1)}, u32[]{:S(2)}, u32[]{:S(2)}) %collective-permute-start.1) | collective-permute-done | bytes 56480 | tf_op jit(solution)/shard_map/ppermute | solution.py:14
  33.2 1.1 collective-permute-done.2
  37.0 0.5 fusion.165
  38.3 5.2 %fusion.171 = (f32[4,3,343]{2,1,0:T(4,128)S(1)}, f32[4,3,343,343]{2,3,1,0:T(8,128)}) fusion(pred[4,343,343]{1,2,0:T(8,128)(4,1)S(1)} %broadcast_compare_fusion, bf16[4,343,3,16]{1,3,2,0:T(8,128)(2,1)S(1)} %bitcast.192, bf16[4,343,3,16]{1,3,2,0:T(8,128)(2,1)S(1)} %bitcast.194), kind=kOutput, calls=%fused_computation.245 | convolution fusion | flops 50824708 | bytes 6397636 | tf_op jit(solution)/shard_map/while/body/eval_jaxpr/sub | solution.py:53
  43.5 3.4 %fusion.19 = bf16[4,343,3,16]{1,3,2,0:T(8,128)(2,1)S(1)} fusion(bf16[4,343,3,16]{1,3,2,0:T(8,128)(2,1)S(1)} %bitcast.195, f32[4,3,343,343]{2,3,1,0:T(8,128)} %get-tuple-element.70, f32[4,3,343]{2,1,0:T(4,128)S(1)} %get-tuple-element.69), kind=kOutput, calls=%fused_computation.56 | convolution fusion | flops 48066648 | bytes 5927040 | tf_op jit(solution)/shard_map/while/body/eval_jaxpr/ghqk,gkhd->gqhd/dot_general | solution.py:56
  46.9 1.2 copy.30
  48.1 0.7 convert_element_type.172
  49.9 0.7 fusion.15
  51.0 0.7 collective-permute-start.3
  52.1 9.4 %collective-permute-done.3 = bf16[4,7,28,48]{3,2,1,0:T(8,128)(2,1)S(1)} collective-permute-done((bf16[4,7,28,48]{3,2,1,0:T(8,128)(2,1)S(1)}, bf16[4,7,28,48]{3,2,1,0:T(8,128)(2,1)S(1)}, u32[]{:S(2)}, u32[]{:S(2)}) %collective-permute-start.3) | collective-permute-done | bytes 75296 | tf_op jit(solution)/shard_map/ppermute | solution.py:14
  61.6 1.5 %collective-permute-start.4 = (bf16[11,4,28,48]{3,2,1,0:T(8,128)(2,1)S(1)}, bf16[11,4,28,48]{3,2,1,0:T(8,128)(2,1)S(1)}, u32[]{:S(2)}, u32[]{:S(2)}) collective-permute-start(bf16[11,4,28,48]{3,2,1,0:T(8,128)(2,1)S(1)} %slice.370), channel_id=1, source_target_pairs={{0,2},{2,0},{1,3},{3,1},{4,6},{6,4},{5,7},{7,5},{8,10},{10,8},{9,1... | collective-permute-start | bytes 354824 | tf_op jit(solution)/shard_map/ppermute | solution.py:14
  63.2 8.4 %collective-permute-done.4 = bf16[11,4,28,48]{3,2,1,0:T(8,128)(2,1)S(1)} collective-permute-done((bf16[11,4,28,48]{3,2,1,0:T(8,128)(2,1)S(1)}, bf16[11,4,28,48]{3,2,1,0:T(8,128)(2,1)S(1)}, u32[]{:S(2)}, u32[]{:S(2)}) %collective-permute-start.4) | collective-permute-done | bytes 118304 | tf_op jit(solution)/shard_map/ppermute | solution.py:14
  71.9 1.2 %collective-permute-done.5 = bf16[11,11,4,48]{3,2,1,0:T(4,128)(2,1)S(1)} collective-permute-done((bf16[11,11,4,48]{3,2,1,0:T(4,128)(2,1)S(1)}, bf16[11,11,4,48]{3,2,1,0:T(4,128)(2,1)S(1)}, u32[]{:S(2)}, u32[]{:S(2)}) %collective-permute-start.5) | collective-permute-done | bytes 46496 | tf_op jit(solution)/shard_map/ppermute | solution.py:14
  74.0 3.3 %fusion.167 = (bf16[7,7,28,48]{3,2,1,0:T(8,128)(2,1)}, bf16[7,7,28,48]{3,2,1,0:T(8,128)(2,1)}, bf16[7,7,28,48]{3,2,1,0:T(8,128)(2,1)}, bf16[7,7,28,48]{3,2,1,0:T...) fusion(bf16[9,9,30,48]{3,2,1,0:T(8,128)(2,1)S(1)} %fusion.40), kind=kLoop, calls=%fused_computation.241 | loop fusion | bytes 5005056 | tf_op jit(solution)/shard_map/slice | solution.py:109
  77.3 0.9 reshape.469
  78.2 0.9 reshape.470
  79.0 0.9 reshape.471
  80.0 0.9 reshape.472
  80.9 0.9 reshape.473
  81.8 0.9 reshape.474
  82.7 0.9 reshape.475
  85.2 1.3 %fusion.112 = f32[1372,48]{0,1:T(8,128)S(1)} fusion(bf16[1372,48]{1,0:T(8,128)(2,1)} %reshape.469, bf16[27,48,48]{2,1,0:T(8,128)(2,1)} %param.14), kind=kOutput, calls=%fused_computation.161 | convolution fusion | flops 6322176 | bytes 627968 | tf_op jit(solution)/shard_map/dot_general | solution.py:110
  86.5 1.3 %convolution_add_fusion.25 = f32[1372,48]{0,1:T(8,128)S(1)} fusion(f32[1372,48]{0,1:T(8,128)S(1)} %fusion.112, bf16[1372,48]{1,0:T(8,128)(2,1)} %reshape.470, bf16[27,48,48]{2,1,0:T(8,128)(2,1)} %param.14), kind=kOutput, calls=%fused_computation.43 | convolution fusion | flops 6388032 | bytes 891392 | tf_op jit(solution)/shard_map/dot_general | solution.py:110
  87.8 1.0 convolution_add_fusion.24
  88.9 1.0 convolution_add_fusion.23
  89.9 1.0 convolution_add_fusion.22
  90.9 1.0 convolution_add_fusion.21
  91.9 1.0 convolution_add_fusion.20
  92.9 1.0 convolution_add_fusion.19
  93.9 1.0 convolution_add_fusion.18
  94.9 1.0 convolution_add_fusion.17
  95.9 1.0 convolution_add_fusion.16
  96.9 1.0 convolution_add_fusion.15
  98.0 1.0 convolution_add_fusion.14
  99.0 1.8 %convolution_add_fusion.13 = f32[1372,48]{0,1:T(8,128)} fusion(f32[1372,48]{0,1:T(8,128)S(1)} %convolution_add_fusion.14, bf16[1372,48]{1,0:T(8,128)(2,1)S(1)} %reshape.468, bf16[27,48,48]{2,1,0:T(8,128)(2,1)} %param.14), kind=kOutput, calls=%fused_computation.31 | convolution fusion | flops 6388032 | bytes 670848 | tf_op jit(solution)/shard_map/dot_general | solution.py:110
  100.8 0.9 reshape.482
  101.7 0.9 reshape.483
  102.6 0.9 reshape.484
  103.5 0.9 reshape.485
  104.3 0.9 reshape.486
  107.0 1.4 %convolution_add_fusion.12 = f32[1372,48]{0,1:T(8,128)S(1)} fusion(f32[1372,48]{0,1:T(8,128)} %convolution_add_fusion.13, bf16[1372,48]{1,0:T(8,128)(2,1)} %reshape.482, bf16[27,48,48]{2,1,0:T(8,128)(2,1)} %param.14), kind=kOutput, calls=%fused_computation.30 | convolution fusion | flops 6388032 | bytes 898304 | tf_op jit(solution)/shard_map/dot_general | solution.py:110
  108.4 1.3 %convolution_add_fusion.11 = f32[1372,48]{0,1:T(8,128)S(1)} fusion(f32[1372,48]{0,1:T(8,128)S(1)} %convolution_add_fusion.12, bf16[1372,48]{1,0:T(8,128)(2,1)} %reshape.483, bf16[27,48,48]{2,1,0:T(8,128)(2,1)} %param.14), kind=kOutput, calls=%fused_computation.29 | convolution fusion | flops 6388032 | bytes 891392 | tf_op jit(solution)/shard_map/dot_general | solution.py:110
  109.7 1.0 convolution_add_fusion.10
  110.7 1.0 convolution_add_fusion.9
  111.7 1.0 convolution_add_fusion.8
  112.7 1.0 convolution_add_fusion.7
  113.7 1.0 convolution_add_fusion.6
  114.7 1.0 convolution_add_fusion.5
  115.7 1.0 convolution_add_fusion.4
  116.7 1.0 convolution_add_fusion.3
  117.7 1.0 convolution_add_fusion.2
  118.7 1.0 convolution_add_fusion.1
  119.7 1.0 fusion.172
  121.2 0.9 reshape.495
  (168 shorter events, 16.3 us)
Async XLA Ops:
  0.0 2.5 %copy-start = (bf16[7,7,28,48]{3,2,1,0:T(8,128)(2,1)S(1)}, bf16[7,7,28,48]{3,2,1,0:T(8,128)(2,1)}, u32[]{:S(2)}) copy-start(bf16[7,7,28,48]{3,2,1,0:T(8,128)(2,1)} %param.8) | copy-start | bytes 395140
  0.0 2.5 %copy-start.30 = (f32[2,2,48]{2,1,0:T(2,128)S(1)}, f32[2,2,48]{2,1,0:T(2,128)}, u32[]{:S(2)}) copy-start(f32[2,2,48]{2,1,0:T(2,128)} %param.13) | copy-start | bytes 2308
  1.4 2.4 %copy-start.28 = (bf16[2,48,144]{2,1,0:T(8,128)(2,1)S(1)}, bf16[2,48,144]{2,1,0:T(8,128)(2,1)}, u32[]{:S(2)}) copy-start(bf16[2,48,144]{2,1,0:T(8,128)(2,1)} %param.9) | copy-start | bytes 82948
  16.4 0.7 copy-start.29
  16.5 1.0 copy-start.32
  16.5 1.0 copy-start.33
  18.5 8.9 %collective-permute-start = (bf16[3,7,28,48]{3,2,1,0:T(8,128)(2,1)S(1)}, bf16[3,7,28,48]{3,2,1,0:T(8,128)(2,1)S(1)}, u32[]{:S(2)}, u32[]{:S(2)}) collective-permute-start(bf16[3,7,28,48]{3,2,1,0:T(8,128)(2,1)S(1)} %slice.284), channel_id=1, source_target_pairs={{0,12},{4,0},{8,4},{12,8},{1,13},{5,1},{9,5},{13,9},{2,14},{6,2},{... | collective-permute-start | bytes 169352 | tf_op jit(solution)/shard_map/ppermute | solution.py:14
  27.5 5.5 %collective-permute-start.1 = (bf16[7,3,28,48]{3,2,1,0:T(8,128)(2,1)S(1)}, bf16[7,3,28,48]{3,2,1,0:T(8,128)(2,1)S(1)}, u32[]{:S(2)}, u32[]{:S(2)}) collective-permute-start(bf16[7,3,28,48]{3,2,1,0:T(8,128)(2,1)S(1)} %slice.363), channel_id=1, source_target_pairs={{0,2},{2,0},{1,3},{3,1},{4,6},{6,4},{5,7},{7,5},{8,10},{10,8},{9,1... | collective-permute-start | bytes 169352 | tf_op jit(solution)/shard_map/ppermute | solution.py:14
  33.0 1.3 %collective-permute-start.2 = (bf16[7,7,3,48]{3,2,1,0:T(4,128)(2,1)S(1)}, bf16[7,7,3,48]{3,2,1,0:T(4,128)(2,1)S(1)}, u32[]{:S(2)}, u32[]{:S(2)}) collective-permute-start(bf16[7,7,3,48]{3,2,1,0:T(4,128)(2,1)S(1)} %pad_maximum_fusion.4), channel_id=1, source_target_pairs={{0,1},{1,0},{2,3},{3,2},{4,5},{5,4},{6,7},{7,6},{8,9},{9,8},{10,11... | collective-permute-start | bytes 42344 | tf_op jit(solution)/shard_map/ppermute | solution.py:14
  51.0 10.5 %collective-permute-start.3 = (bf16[4,7,28,48]{3,2,1,0:T(8,128)(2,1)S(1)}, bf16[4,7,28,48]{3,2,1,0:T(8,128)(2,1)S(1)}, u32[]{:S(2)}, u32[]{:S(2)}) collective-permute-start(bf16[4,7,28,48]{3,2,1,0:T(8,128)(2,1)S(1)} %slice.299), channel_id=1, source_target_pairs={{0,4},{4,8},{8,12},{12,0},{1,5},{5,9},{9,13},{13,1},{2,6},{6,10},{... | collective-permute-start | bytes 225800 | tf_op jit(solution)/shard_map/ppermute | solution.py:14
  61.6 10.0 %collective-permute-start.4 = (bf16[11,4,28,48]{3,2,1,0:T(8,128)(2,1)S(1)}, bf16[11,4,28,48]{3,2,1,0:T(8,128)(2,1)S(1)}, u32[]{:S(2)}, u32[]{:S(2)}) collective-permute-start(bf16[11,4,28,48]{3,2,1,0:T(8,128)(2,1)S(1)} %slice.370), channel_id=1, source_target_pairs={{0,2},{2,0},{1,3},{3,1},{4,6},{6,4},{5,7},{7,5},{8,10},{10,8},{9,1... | collective-permute-start | bytes 354824 | tf_op jit(solution)/shard_map/ppermute | solution.py:14
  71.7 1.4 %collective-permute-start.5 = (bf16[11,11,4,48]{3,2,1,0:T(4,128)(2,1)S(1)}, bf16[11,11,4,48]{3,2,1,0:T(4,128)(2,1)S(1)}, u32[]{:S(2)}, u32[]{:S(2)}) collective-permute-start(bf16[11,11,4,48]{3,2,1,0:T(4,128)(2,1)S(1)} %pad_maximum_fusion.3), channel_id=1, source_target_pairs={{0,1},{1,0},{2,3},{3,2},{4,5},{5,4},{6,7},{7,6},{8,9},{9,8},{10,11... | collective-permute-start | bytes 139400 | tf_op jit(solution)/shard_map/ppermute | solution.py:14
  80.0 3.6 %copy-start.19 = (bf16[7,7,28,48]{3,2,1,0:T(8,128)(2,1)S(1)}, bf16[7,7,28,48]{3,2,1,0:T(8,128)(2,1)}, u32[]{:S(2)}) copy-start(bf16[7,7,28,48]{3,2,1,0:T(8,128)(2,1)} %get-tuple-element.52) | copy-start | bytes 395140
  80.9 2.8 %copy-start.18 = (bf16[7,7,28,48]{3,2,1,0:T(8,128)(2,1)S(1)}, bf16[7,7,28,48]{3,2,1,0:T(8,128)(2,1)}, u32[]{:S(2)}) copy-start(bf16[7,7,28,48]{3,2,1,0:T(8,128)(2,1)} %get-tuple-element.51) | copy-start | bytes 395140
  81.8 2.1 %copy-start.17 = (bf16[7,7,28,48]{3,2,1,0:T(8,128)(2,1)S(1)}, bf16[7,7,28,48]{3,2,1,0:T(8,128)(2,1)}, u32[]{:S(2)}) copy-start(bf16[7,7,28,48]{3,2,1,0:T(8,128)(2,1)} %get-tuple-element.50) | copy-start | bytes 395140
  82.7 1.3 %copy-start.16 = (bf16[7,7,28,48]{3,2,1,0:T(8,128)(2,1)S(1)}, bf16[7,7,28,48]{3,2,1,0:T(8,128)(2,1)}, u32[]{:S(2)}) copy-start(bf16[7,7,28,48]{3,2,1,0:T(8,128)(2,1)} %get-tuple-element.49) | copy-start | bytes 395140
  83.5 1.0 copy-start.15
  83.7 1.0 copy-start.14
  84.9 2.9 %copy-start.24 = (bf16[1372,48]{1,0:T(8,128)(2,1)S(1)}, bf16[1372,48]{1,0:T(8,128)(2,1)}, u32[]{:S(2)}) copy-start(bf16[1372,48]{1,0:T(8,128)(2,1)} %reshape.471) | copy-start | bytes 395140
  85.0 3.8 %copy-start.23 = (bf16[1372,48]{1,0:T(8,128)(2,1)S(1)}, bf16[1372,48]{1,0:T(8,128)(2,1)}, u32[]{:S(2)}) copy-start(bf16[1372,48]{1,0:T(8,128)(2,1)} %reshape.472) | copy-start | bytes 395140
  86.5 3.5 %copy-start.22 = (bf16[1372,48]{1,0:T(8,128)(2,1)S(1)}, bf16[1372,48]{1,0:T(8,128)(2,1)}, u32[]{:S(2)}) copy-start(bf16[1372,48]{1,0:T(8,128)(2,1)} %reshape.473) | copy-start | bytes 395140
  87.8 3.1 %copy-start.21 = (bf16[1372,48]{1,0:T(8,128)(2,1)S(1)}, bf16[1372,48]{1,0:T(8,128)(2,1)}, u32[]{:S(2)}) copy-start(bf16[1372,48]{1,0:T(8,128)(2,1)} %reshape.474) | copy-start | bytes 395140
  88.9 3.1 %copy-start.20 = (bf16[1372,48]{1,0:T(8,128)(2,1)S(1)}, bf16[1372,48]{1,0:T(8,128)(2,1)}, u32[]{:S(2)}) copy-start(bf16[1372,48]{1,0:T(8,128)(2,1)} %reshape.475) | copy-start | bytes 395140
  96.9 3.9 %copy-start.13 = (bf16[7,7,28,48]{3,2,1,0:T(8,128)(2,1)S(1)}, bf16[7,7,28,48]{3,2,1,0:T(8,128)(2,1)}, u32[]{:S(2)}) copy-start(bf16[7,7,28,48]{3,2,1,0:T(8,128)(2,1)} %get-tuple-element.46) | copy-start | bytes 395140
  98.0 3.7 %copy-start.12 = (bf16[7,7,28,48]{3,2,1,0:T(8,128)(2,1)S(1)}, bf16[7,7,28,48]{3,2,1,0:T(8,128)(2,1)}, u32[]{:S(2)}) copy-start(bf16[7,7,28,48]{3,2,1,0:T(8,128)(2,1)} %get-tuple-element.45) | copy-start | bytes 395140
  99.0 3.6 %copy-start.11 = (bf16[7,7,28,48]{3,2,1,0:T(8,128)(2,1)S(1)}, bf16[7,7,28,48]{3,2,1,0:T(8,128)(2,1)}, u32[]{:S(2)}) copy-start(bf16[7,7,28,48]{3,2,1,0:T(8,128)(2,1)} %get-tuple-element.44) | copy-start | bytes 395140
  99.0 4.4 %copy-start.10 = (bf16[7,7,28,48]{3,2,1,0:T(8,128)(2,1)S(1)}, bf16[7,7,28,48]{3,2,1,0:T(8,128)(2,1)}, u32[]{:S(2)}) copy-start(bf16[7,7,28,48]{3,2,1,0:T(8,128)(2,1)} %get-tuple-element.43) | copy-start | bytes 395140
  100.8 3.5 %copy-start.9 = (bf16[7,7,28,48]{3,2,1,0:T(8,128)(2,1)S(1)}, bf16[7,7,28,48]{3,2,1,0:T(8,128)(2,1)}, u32[]{:S(2)}) copy-start(bf16[7,7,28,48]{3,2,1,0:T(8,128)(2,1)} %get-tuple-element.42) | copy-start | bytes 395140
  101.7 3.5 %copy-start.8 = (bf16[7,7,28,48]{3,2,1,0:T(8,128)(2,1)S(1)}, bf16[7,7,28,48]{3,2,1,0:T(8,128)(2,1)}, u32[]{:S(2)}) copy-start(bf16[7,7,28,48]{3,2,1,0:T(8,128)(2,1)} %get-tuple-element.41) | copy-start | bytes 395140
  102.6 2.8 %copy-start.7 = (bf16[7,7,28,48]{3,2,1,0:T(8,128)(2,1)S(1)}, bf16[7,7,28,48]{3,2,1,0:T(8,128)(2,1)}, u32[]{:S(2)}) copy-start(bf16[7,7,28,48]{3,2,1,0:T(8,128)(2,1)} %get-tuple-element.40) | copy-start | bytes 395140
  103.5 2.1 %copy-start.6 = (bf16[7,7,28,48]{3,2,1,0:T(8,128)(2,1)S(1)}, bf16[7,7,28,48]{3,2,1,0:T(8,128)(2,1)}, u32[]{:S(2)}) copy-start(bf16[7,7,28,48]{3,2,1,0:T(8,128)(2,1)} %get-tuple-element.39) | copy-start | bytes 395140
  104.3 1.4 %copy-start.5 = (bf16[7,7,28,48]{3,2,1,0:T(8,128)(2,1)S(1)}, bf16[7,7,28,48]{3,2,1,0:T(8,128)(2,1)}, u32[]{:S(2)}) copy-start(bf16[7,7,28,48]{3,2,1,0:T(8,128)(2,1)} %get-tuple-element.38) | copy-start | bytes 395140
  105.3 1.0 copy-start.4
  105.4 1.0 copy-start.3
  105.6 1.1 copy-start.2
  105.7 1.1 copy-start.1
  107.0 2.8 %copy-start.27 = (bf16[1372,48]{1,0:T(8,128)(2,1)S(1)}, bf16[1372,48]{1,0:T(8,128)(2,1)}, u32[]{:S(2)}) copy-start(bf16[1372,48]{1,0:T(8,128)(2,1)} %reshape.484) | copy-start | bytes 395140
  107.0 3.8 %copy-start.26 = (bf16[1372,48]{1,0:T(8,128)(2,1)S(1)}, bf16[1372,48]{1,0:T(8,128)(2,1)}, u32[]{:S(2)}) copy-start(bf16[1372,48]{1,0:T(8,128)(2,1)} %reshape.485) | copy-start | bytes 395140
  108.4 3.3 %copy-start.25 = (bf16[1372,48]{1,0:T(8,128)(2,1)S(1)}, bf16[1372,48]{1,0:T(8,128)(2,1)}, u32[]{:S(2)}) copy-start(bf16[1372,48]{1,0:T(8,128)(2,1)} %reshape.486) | copy-start | bytes 395140
  117.7 3.1 %copy-start.31 = (f32[48]{0:T(128)S(1)}, f32[48]{0:T(128)}, u32[]{:S(2)}) copy-start(f32[48]{0:T(128)} %param.15) | copy-start | bytes 580
where the time goes:
time: 124 us; the launch traced here: 122 us
  matrix products  48.5 us (39%)
  local copies, waits for them, and re-layouts  31 us (25%)
  waiting for transfers between devices  26.6 us (21%)
  starting transfers between devices  9.24 us (7%)
  other arithmetic  5.52 us (4%)
  between operations  1.25 us (1%)
    dot_general x27, matrix products, conv_out(): jnp.dot(piece, conv_weight[tap], preferred_element_type=jnp.float32)  29 us
    ppermute x6, waiting for transfers between devices, shifted(): return lax.ppermute(value, axis, pairs)  26.6 us
    reshape x26, local copies, waits for them, and re-layouts, conv_out(): piece = padded[dx:dx + sx, dy:dy + sy, dz:dz + sz].reshape(-1, width)  12.5 us
    sub x2, matrix products, attend_group(): scores = scores - jnp.max(scores, -1, keepdims=True)  10 us
    ppermute x6, starting transfers between devices, shifted(): return lax.ppermute(value, axis, pairs)  9.24 us
    dot_general x2, matrix products, attend_group(): jnp.einsum('ghqk,gkhd->gqhd', probs, vals, preferred_element_type=jnp.flo...  6.86 us
    slice x2, local copies, waits for them, and re-layouts, conv_out(): piece = padded[dx:dx + sx, dy:dy + sy, dz:dz + sz].reshape(-1, width)  3.78 us
    convert_element_type x4, local copies, waits for them, and re-layouts, attend_group(): return mixed.reshape(group, count, width).astype(jnp.bfloat16)  3.69 us
  transfers between devices with their start and end apart: 6, of which 6 were waited for; matrix products, arithmetic and copies ran while one was open for 1% of the time, Pallas kernels for 0%

commit v1 on v0

v1 whole, which is shorter than its diff:
```python
import functools
import itertools

import jax
import jax.numpy as jnp
import numpy as np
from jax import lax
from jax.experimental import pallas as pl
from jax.experimental.pallas import tpu as pltpu
from jax.sharding import PartitionSpec as P

HEADS = 3
WINDOW = 7
SHIFT = 3
LANE = 128
TILES = 3
LANES = TILES * LANE
MESH = pl.DeviceIdType.MESH
F32 = jnp.float32
BF16 = jnp.bfloat16


def column_lanes():
    low, high = range(SHIFT), range(SHIFT, WINDOW)
    both = list(itertools.product(low, low))
    first = list(itertools.product(low, high)) + both[:6]
    second = list(itertools.product(high, low)) + both[6:]
    groups = (list(itertools.product(high, high)), first, second)
    place = {}
    for tile, group in enumerate(groups):
        for at, column in enumerate(group):
            place[column] = tile * LANE + at * WINDOW
    return place


PLACE = column_lanes()


def lane_facts():
    facts = np.zeros((8, LANES), np.int32)
    for (x, y), lane in PLACE.items():
        for z in range(WINDOW):
            facts[0, lane + z] = x < SHIFT
            facts[1, lane + z] = y < SHIFT
            facts[2, lane + z] = z < SHIFT
            facts[3, lane + z] = 1
    return facts


def norm_columns(values, gain):
    mean = jnp.mean(values, 0, keepdims=True)
    centred = values - mean
    spread = jnp.mean(centred * centred, 0, keepdims=True)
    return centred * lax.rsqrt(spread + 1e-05) * gain


def norm_rows(values, gain):
    mean = jnp.mean(values, -1, keepdims=True)
    centred = values - mean
    spread = jnp.mean(centred * centred, -1, keepdims=True)
    return centred * lax.rsqrt(spread + 1e-05) * gain


def dot(a, b):
    return jnp.dot(a, b, preferred_element_type=F32)


def block(state, key_mask, query_mask, w_qkv, w_proj, w_up, w_down, gain0, gain1):
    width = state.shape[0]
    depth = width // HEADS
    normed = norm_columns(state, gain0).astype(BF16)
    qkv = dot(w_qkv, normed)
    scale = depth ** (-0.5) * np.log2(np.e)
    query = (qkv[:width] * scale).astype(BF16)
    keys = qkv[width : 2 * width].astype(BF16)
    vals = qkv[2 * width :].astype(BF16)
    ones = jnp.ones((16, LANES), BF16)
    mixed = []
    for head in range(HEADS):
        rows = slice(head * depth, (head + 1) * depth)
        q = jnp.concatenate([query[rows], query_mask], 0)
        k = jnp.concatenate([keys[rows], key_mask], 0)
        scores = lax.dot_general(k, q, (((0,), (0,)), ((), ())), preferred_element_type=F32)
        top = jnp.max(scores, 0, keepdims=True)
        weights = jnp.exp2(scores - top).astype(BF16)
        both = dot(jnp.concatenate([vals[rows], ones], 0), weights)
        mixed.append(both[:depth] / both[depth : depth + 1])
    mixed = jnp.concatenate(mixed, 0).astype(BF16)
    state = (state + dot(w_proj, mixed)).astype(BF16).astype(F32)
    normed = norm_columns(state, gain1).astype(BF16)
    upper = jax.nn.gelu(dot(w_up, normed)).astype(BF16)
    return (state + dot(w_down, upper)).astype(BF16)


def kernel(
    sizes, facts_ref, vol_ref, wqkv_ref, wproj_ref, wup_ref, wdown_ref, gain_ref, cw_ref, cg_ref,
    out_ref, wide, win, r1, r2, tqkv, tproj, tup, tdown, tgain, rows_s, pad, cols, cw, ys,
    send1, recv1, send2, recv2,
):
    sx, sy, sz, width = sizes
    nwin = sz // WINDOW
    axes = ("gx", "gy", "gz")
    here = [lax.axis_index(a) for a in axes]
    count = [lax.axis_size(a) for a in axes]

    def device(steps, sign):
        return {
            a: lax.rem(here[i] + sign * steps[i] + count[i], count[i]) for i, a in enumerate(axes)
        }

    others = [s for s in itertools.product((0, 1), repeat=3) if any(s)]
    barrier = pltpu.get_barrier_semaphore()
    for steps in others:
        for sign in (-1, 1):
            pl.semaphore_signal(barrier, inc=1, device_id=device(steps, sign), device_id_type=MESH)

    for b in range(2):
        tqkv[b] = wqkv_ref[b].astype(F32).T.astype(BF16)
        tproj[b] = wproj_ref[b].astype(F32).T.astype(BF16)
        tup[b] = wup_ref[b].astype(F32).T.astype(BF16)
        tdown[b] = wdown_ref[b].astype(F32).T.astype(BF16)
        for i in range(2):
            wide_gain = jnp.broadcast_to(gain_ref[b, i : i + 1, :], (LANE, width)).T
            tgain[b, i] = jnp.concatenate([wide_gain] * TILES, 1)
    for dy in range(3):
        for dz in range(3):
            cw[dy, dz * width : (dz + 1) * width, :] = jnp.concatenate(
                [cw_ref[9 * dx + 3 * dy + dz].astype(F32) for dx in range(3)], 1
            ).astype(BF16)

    win[...] = jnp.zeros_like(win)
    wide[:, :sz, :] = vol_ref[...].reshape(sx * sy, sz, width).astype(F32)

    def gather(w, carry):
        for (x, y), lane in PLACE.items():
            win[w, pl.ds(lane, WINDOW), :] = wide[x * sy + y, pl.ds(w * WINDOW, WINDOW), :]
        return carry

    lax.fori_loop(0, nwin, gather, 0)

    xlow, ylow, zlow, valid = [facts_ref[i : i + 1, :] for i in range(4)]
    last = [jnp.where(here[i] == count[i] - 1, 1, 0) for i in range(3)]
    row = lax.broadcasted_iota(jnp.int32, (16, LANES), 0)

    def masks(code):
        key = jnp.where(row == 8, 1 - valid, jnp.where(row == code, valid, 0))
        query = jnp.where(row == code, 0.0, jnp.where(row <= 8, -1e30, 0.0))
        return key.astype(F32).astype(BF16), query.astype(BF16)

    def labels(w):
        edge = last[2] * jnp.where(w == nwin - 1, 1, 0)
        return masks(4 * last[0] * xlow + 2 * last[1] * ylow + edge * zlow)

    def weights(b):
        return tqkv[b], tproj[b], tup[b], tdown[b], tgain[b, 0], tgain[b, 1]

    def put(ref, at, value):
        for tile in range(TILES):
            ref[0, at, tile] = value[:, tile * LANE : (tile + 1) * LANE]

    spans = {0: (0, 1), 1: (1, 1), 2: (2, 1), 3: (1, 2)}

    def copies1(w, across):
        found = []
        for source in range(0 if across else 1, 4):
            start, size = spans[source]
            steps = (source % 2, source // 2, 1 if across else 0)
            sem = 3 * nwin + source if across else 3 * w + source - 1
            found.append(
                pltpu.make_async_remote_copy(
                    src_ref=r1.at[0, w, pl.ds(start, size)],
                    dst_ref=r1.at[source, nwin if across else w, pl.ds(start, size)],
                    send_sem=send1.at[sem],
                    recv_sem=recv1.at[sem],
                    device_id=device(steps, -1),
                    device_id_type=MESH,
                )
            )
        return found

    def copies2(w, across):
        found = []
        for source in range(0 if across else 1, 4):
            steps = (source % 2, source // 2, 1 if across else 0)
            sem = 3 * nwin + source if across else 3 * w + source - 1
            found.append(
                pltpu.make_async_remote_copy(
                    src_ref=r2.at[0, w + 1],
                    dst_ref=r2.at[source, 0 if across else w + 1],
                    send_sem=send2.at[sem],
                    recv_sem=recv2.at[sem],
                    device_id=device(steps, 1),
                    device_id_type=MESH,
                )
            )
        return found

    plain_key, plain_query = masks(jnp.zeros((1, LANES), jnp.int32))

    def first(i, carry):
        w = lax.rem(i + nwin - 1, nwin)
        out = block(win[w].T, plain_key, plain_query, *weights(0))
        put(r1, w, out)

        @pl.when(i == 0)
        def _():
            pl.semaphore_wait(barrier, 2 * len(others))

        for copy in copies1(w, False):
            copy.start()

        @pl.when(w == 0)
        def _():
            for copy in copies1(0, True):
                copy.start()

        return carry

    lax.fori_loop(0, nwin, first, 0)

    def natural1(j):
        both = (xlow * ylow) == 1
        one = both[:, LANE : 2 * LANE]
        two = both[:, 2 * LANE :]
        return jnp.concatenate(
            [
                r1[0, j, 0].astype(F32),
                jnp.where(one, r1[3, j, 1].astype(F32), r1[1, j, 1].astype(F32)),
                jnp.where(two, r1[3, j, 2].astype(F32), r1[2, j, 2].astype(F32)),
            ],
            1,
        )

    for w in range(nwin):
        for copy in copies1(w, False):
            copy.wait()
    for copy in copies1(0, True):
        copy.wait()

    def second(i, carry):
        w = lax.rem(i + nwin - 1, nwin)
        state = jnp.where(zlow == 1, natural1(w + 1), natural1(w))
        key_mask, query_mask = labels(w)
        out = block(state, key_mask, query_mask, *weights(1))
        put(r2, w + 1, out)
        for copy in copies2(w, False):
            copy.start()

        @pl.when(w == nwin - 1)
        def _():
            for copy in copies2(nwin - 1, True):
                copy.start()

        return carry

    lax.fori_loop(0, nwin, second, 0)

    for w in range(nwin):
        for copy in copies2(w, False):
            copy.wait()
    for copy in copies2(nwin - 1, True):
        copy.wait()

    py = sy + 2

    def spread(jj, carry):
        high_at = lax.rem(jj, nwin + 1)
        low_at = lax.rem(jj + nwin, nwin + 1)
        outer = jnp.where((jj == 0) | (jj == nwin + 1), 1, 0)
        above = jnp.where(here[2] < count[2] - 1, 1, 0)
        below = jnp.where(here[2] > 0, 1, 0)
        keep = jnp.where(zlow == 1, jnp.maximum(above, 1 - outer), jnp.maximum(below, 1 - outer))
        for source in range(4):
            tiles = []
            for tile in range(TILES):
                part = slice(tile * LANE, (tile + 1) * LANE)
                value = jnp.where(
                    zlow[:, part] == 1,
                    r2[source, low_at, tile].astype(F32),
                    r2[source, high_at, tile].astype(F32),
                )
                tiles.append(jnp.where(keep[:, part] == 1, value, 0.0))
            rows_s[source] = jnp.concatenate(tiles, 1).T
        for x in range(-1, sx + 1):
            for y in range(-1, sy + 1):
                ok = None
                fromx = x < SHIFT
                fromy = y < SHIFT
                for at, axis, size in ((x, 0, sx), (y, 1, sy)):
                    if at == -1:
                        test = here[axis] > 0
                    elif at == size:
                        test = here[axis] < count[axis] - 1
                    else:
                        continue
                    ok = test if ok is None else ok & test
                source = int(fromx) + 2 * int(fromy)
                lane = PLACE[x % WINDOW, y % WINDOW]
                value = rows_s[source, pl.ds(lane, WINDOW), :]
                if ok is not None:
                    value = jnp.where(ok, value, 0.0)
                pad[(x + 1) * py + y + 1, pl.ds(1 + WINDOW * jj, WINDOW), :] = value
        return carry

    lax.fori_loop(0, nwin + 2, spread, 0)

    deep = cols.shape[1]

    def stack(xp, carry):
        for y in range(py):
            at = xp * py + y
            cols[at] = jnp.concatenate(
                [pad[at, WINDOW + dz : WINDOW + dz + deep, :] for dz in range(3)], 1
            ).astype(BF16)
        total = None
        for dy in range(3):
            piece = cols[pl.ds(xp * py + dy, sy)].reshape(sy * deep, 3 * width)
            part = dot(piece, cw[dy])
            total = part if total is None else total + part
        ys[xp] = total
        return carry

    lax.fori_loop(0, sx + 2, stack, 0)

    def finish(x, carry):
        total = (
            ys[x][:, :width] + ys[x + 1][:, width : 2 * width] + ys[x + 2][:, 2 * width : 3 * width]
        )
        value = norm_rows(total, cg_ref[...])
        value = jnp.where(value >= 0, value, 0.01 * value).reshape(sy, deep, width)
        centre = pad[pl.ds((x + 1) * py + 1, sy), WINDOW + 1 : WINDOW + 1 + deep, :]
        out_ref[x] = (centre + value)[:, :sz].astype(BF16)
        return carry

    lax.fori_loop(0, sx, finish, 0)


def body(volume, w_qkv, w_proj, w_up, w_down, norm_gain, conv_weight, conv_gain):
    sx, sy, sz, width = volume.shape
    assert sx == WINDOW and sy == WINDOW and sz % WINDOW == 0
    nwin = sz // WINDOW
    hidden = w_up.shape[-1]
    deep = -(-sz // 16) * 16
    tall = -(-(WINDOW + 2 + max(deep, sz + WINDOW)) // 8) * 8
    ncopy = 3 * nwin + 4
    padded = (sx + 2) * (sy + 2)
    vmem = pl.BlockSpec(memory_space=pltpu.VMEM)
    sems = [pltpu.SemaphoreType.DMA((ncopy,))] * 4
    return pl.pallas_call(
        functools.partial(kernel, (sx, sy, sz, width)),
        out_shape=jax.ShapeDtypeStruct(volume.shape, BF16),
        in_specs=[vmem] * 9,
        out_specs=vmem,
        scratch_shapes=[
            pltpu.VMEM((sx * sy, deep, width), F32),
            pltpu.VMEM((nwin, LANES, width), F32),
            pltpu.VMEM((4, nwin + 1, TILES, width, LANE), BF16),
            pltpu.VMEM((4, nwin + 1, TILES, width, LANE), BF16),
            pltpu.VMEM((2, 3 * width, width), BF16),
            pltpu.VMEM((2, width, width), BF16),
            pltpu.VMEM((2, hidden, width), BF16),
            pltpu.VMEM((2, width, hidden), BF16),
            pltpu.VMEM((2, 2, width, LANES), F32),
            pltpu.VMEM((4, LANES, width), F32),
            pltpu.VMEM((padded, tall, width), F32),
            pltpu.VMEM((padded, deep, 3 * width), BF16),
            pltpu.VMEM((3, 3 * width, 3 * width), BF16),
            pltpu.VMEM((sx + 2, sy * deep, 3 * width), F32),
        ]
        + sems,
        compiler_params=pltpu.CompilerParams(
            collective_id=0, has_side_effects=True, vmem_limit_bytes=48 * 1024 * 1024
        ),
    )(
        jnp.asarray(lane_facts()), volume, w_qkv, w_proj, w_up, w_down, norm_gain, conv_weight,
        conv_gain.reshape(1, width),
    )


def solution(mesh):
    placed = (P(("parts", "gx"), "gy", "gz", None), P(), P(), P(), P(), P(), P(), P())
    return jax.shard_map(
        body,
        mesh=mesh,
        in_specs=placed,
        out_specs=P(("parts", "gx"), "gy", "gz", None),
        check_vma=False,
    )
```

time: 124 us -> 39.8 us (0.32); the launches traced: 122 us -> 39.6 us
  matrix products: 48.5 us -> 0 us
  Pallas kernels: 0 us -> 35.8 us
  local copies, waits for them, and re-layouts: 31 us -> 3.7 us
  waiting for transfers between devices: 26.6 us -> 0 us
  starting transfers between devices: 9.24 us -> 0 us
  other arithmetic: 5.52 us -> 0 us
    dot_general x35 -> x0, matrix products: 38.4 us -> none  [the longest x27 29 us: conv_out(): jnp.dot(piece, conv_weight[tap], preferred_element_type=jnp.float32)]
    pallas_call x0 -> x1, Pallas kernels: none -> 35.8 us  [body(): pl.pallas_call(functools.partial(kernel, (sx, sy, sz, width)), out_shape=...]
    ppermute x6 -> x0, waiting for transfers between devices: 26.6 us -> none  [shifted(): return lax.ppermute(value, axis, pairs)]
    reshape x31 -> x0, local copies, waits for them, and re-layouts: 13.9 us -> none  [the longest x26 12.5 us: conv_out(): piece = padded[dx:dx + sx, dy:dy + sy, dz:dz + sz].reshape(-1, width)]
    sub x2 -> x0, matrix products: 10 us -> none  [attend_group(): scores = scores - jnp.max(scores, -1, keepdims=True)]
    ppermute x6 -> x0, starting transfers between devices: 9.24 us -> none  [shifted(): return lax.ppermute(value, axis, pairs)]
    slice x22 -> x0, local copies, waits for them, and re-layouts: 7.32 us -> none  [the longest x2 3.78 us: conv_out(): piece = padded[dx:dx + sx, dy:dy + sy, dz:dz + sz].reshape(-1, width)]
    convert_element_type x13 -> x0, local copies, waits for them, and re-layouts: 6.48 us -> none  [the longest x4 3.69 us: attend_group(): return mixed.reshape(group, count, width).astype(jnp.bfloat16)]
  transfers between devices with their start and end apart: 6 -> 0, of which waited for: 6 -> 0; matrix products, arithmetic and copies ran while one was open for 1% -> 0% of each run, Pallas kernels for 0% -> 0%
where the time goes in v1:
time: 39.8 us; the launch traced here: 39.6 us
  Pallas kernels  35.8 us (90%)
  local copies, waits for them, and re-layouts  3.7 us (9%)
    pallas_call x1, Pallas kernels, body(): pl.pallas_call(functools.partial(kernel, (sx, sy, sz, width)), out_shape=...  35.8 us
    unnamed x18, local copies, waits for them, and re-layouts  3.7 us

profile of v1, /device:TPU:0, one launch (start us, length us, event | category | flops | bytes accessed | tf_op | source)
XLA Modules:
  0.0 39.6 jit_solution(8024377829878323917)
XLA Ops:
  0.0 0.0 copy-start.2
  0.0 0.0 copy-start.3
  0.0 0.0 copy-start.4
  0.0 0.0 copy-start.5
  0.0 0.0 copy-start.6
  0.0 0.0 copy-start.7
  0.0 1.0 %copy.10.wdown_ref = bf16[2,192,48]{2,1,0:T(8,128)(2,1)S(1)} copy(bf16[2,192,48]{1,2,0:T(8,128)(2,1)} %param.13) | data formatting | bytes 73728 | tf_op args[4]
  1.0 0.0 copy-done.2
  1.0 0.0 copy-done.3
  1.0 0.0 copy-done.4
  1.0 0.0 copy-done.5
  1.0 0.0 copy-done.6
  1.0 0.0 copy-done.7
  1.0 0.0 copy-start
  1.1 1.0 %copy-done = bf16[7,7,28,48]{3,2,1,0:T(8,128)(2,1)S(1)} copy-done((bf16[7,7,28,48]{3,2,1,0:T(8,128)(2,1)S(1)}, bf16[7,7,28,48]{3,2,1,0:T(8,128)(2,1)}, u32[]{:S(2)}) %copy-start) | copy-done | bytes 131736
  2.0 0.0 copy-start.1
  2.0 1.0 %copy-done.1 = bf16[27,48,48]{2,1,0:T(8,128)(2,1)S(1)} copy-done((bf16[27,48,48]{2,1,0:T(8,128)(2,1)S(1)}, bf16[27,48,48]{2,1,0:T(8,128)(2,1)}, u32[]{:S(2)}) %copy-start.1) | copy-done | bytes 124440
  3.0 35.8 %shard_map.91 = bf16[7,7,28,48]{3,2,1,0:T(8,128)(2,1)S(1)} custom-call(s32[8,384]{1,0:T(8,128)S(1)} %copy-done.5, bf16[7,7,28,48]{3,2,1,0:T(8,128)(2,1)S(1)} %copy-done, bf16[2,48,144]{2,1,0:T(8,128)(2,1)S(1)} %copy-done.2, bf16[2,48,48]{2,1,0:T(8,128)(2,1)S(1)} %copy-done.4, bf16[2,48,192]{2,1,0:T(8,128)(2,1)S(1)} %copy-done.3, ...), custom_call_target="tpu_custom_call" | custom-call | tf_op jit(solution)/shard_map/pallas_call | solution.py:349
  38.8 0.8 %copy.12 = bf16[7,7,28,48]{3,2,1,0:T(8,128)(2,1)} copy(bf16[7,7,28,48]{3,2,1,0:T(8,128)(2,1)S(1)} %shard_map.91) | data formatting | bytes 263424
Async XLA Ops:
  0.0 1.0 %copy-start.2 = (bf16[2,48,144]{2,1,0:T(8,128)(2,1)S(1)}, bf16[2,48,144]{2,1,0:T(8,128)(2,1)}, u32[]{:S(2)}) copy-start(bf16[2,48,144]{2,1,0:T(8,128)(2,1)} %wqkv_ref.1) | copy-start | bytes 82948
  0.0 1.0 %copy-start.3 = (bf16[2,48,192]{2,1,0:T(8,128)(2,1)S(1)}, bf16[2,48,192]{2,1,0:T(8,128)(2,1)}, u32[]{:S(2)}) copy-start(bf16[2,48,192]{2,1,0:T(8,128)(2,1)} %wup_ref.1) | copy-start | bytes 110596
  0.0 1.0 %copy-start.4 = (bf16[2,48,48]{2,1,0:T(8,128)(2,1)S(1)}, bf16[2,48,48]{2,1,0:T(8,128)(2,1)}, u32[]{:S(2)}) copy-start(bf16[2,48,48]{2,1,0:T(8,128)(2,1)} %wproj_ref.1) | copy-start | bytes 27652
  0.0 1.0 %copy-start.5 = (s32[8,384]{1,0:T(8,128)S(1)}, s32[8,384]{1,0:T(8,128)}, u32[]{:S(2)}) copy-start(s32[8,384]{1,0:T(8,128)} %constant.2.clone.facts_ref) | copy-start | bytes 36868
  0.0 1.0 %copy-start.6 = (f32[2,2,48]{2,1,0:T(2,128)S(1)}, f32[2,2,48]{2,1,0:T(2,128)}, u32[]{:S(2)}) copy-start(f32[2,2,48]{2,1,0:T(2,128)} %gain_ref.1) | copy-start | bytes 2308
  0.0 1.0 %copy-start.7 = (f32[48]{0:T(128)S(1)}, f32[48]{0:T(128)}, u32[]{:S(2)}) copy-start(f32[48]{0:T(128)} %param.16) | copy-start | bytes 580
  1.0 1.0 %copy-start = (bf16[7,7,28,48]{3,2,1,0:T(8,128)(2,1)S(1)}, bf16[7,7,28,48]{3,2,1,0:T(8,128)(2,1)}, u32[]{:S(2)}) copy-start(bf16[7,7,28,48]{3,2,1,0:T(8,128)(2,1)} %vol_ref.1) | copy-start | bytes 395140
  2.0 1.0 %copy-start.1 = (bf16[27,48,48]{2,1,0:T(8,128)(2,1)S(1)}, bf16[27,48,48]{2,1,0:T(8,128)(2,1)}, u32[]{:S(2)}) copy-start(bf16[27,48,48]{2,1,0:T(8,128)(2,1)} %cw_ref.1) | copy-start | bytes 373252

commit v2 on v1

--- a/solution.py
+++ b/solution.py
@@ -93,10 +93,20 @@
 
 
 def kernel(
-    sizes, facts_ref, vol_ref, wqkv_ref, wproj_ref, wup_ref, wdown_ref, gain_ref, cw_ref, cg_ref,
-    out_ref, wide, win, r1, r2, tqkv, tproj, tup, tdown, tgain, rows_s, pad, cols, cw, ys,
-    send1, recv1, send2, recv2,
+    sizes, facts_in, vol_in, wqkv_in, wproj_in, wup_in, tdown_in, gain_in, cw_in, cg_in,
+    out_ref, facts_ref, vol_ref, wqkv_ref, wproj_ref, wup_ref, tdown, gain_ref, cw_ref, cg_ref,
+    wide, win, r1, r2, tqkv, tproj, tup, tgain, rows_s, pad, cols, cw, ys,
+    send1, recv1, send2, recv2, loaded,
 ):
+    pairs = (
+        (vol_in, vol_ref), (wqkv_in, wqkv_ref), (wproj_in, wproj_ref), (wup_in, wup_ref),
+        (gain_in, gain_ref), (tdown_in, tdown), (facts_in, facts_ref), (cg_in, cg_ref),
+        (cw_in, cw_ref),
+    )
+    loads = [pltpu.make_async_copy(a, b, loaded.at[i]) for i, (a, b) in enumerate(pairs)]
+    for load in loads:
+        load.start()
+
     sx, sy, sz, width = sizes
     nwin = sz // WINDOW
     axes = ("gx", "gy", "gz")
@@ -114,21 +124,17 @@
         for sign in (-1, 1):
             pl.semaphore_signal(barrier, inc=1, device_id=device(steps, sign), device_id_type=MESH)
 
+    for load in loads[1:8]:
+        load.wait()
     for b in range(2):
         tqkv[b] = wqkv_ref[b].astype(F32).T.astype(BF16)
         tproj[b] = wproj_ref[b].astype(F32).T.astype(BF16)
         tup[b] = wup_ref[b].astype(F32).T.astype(BF16)
-        tdown[b] = wdown_ref[b].astype(F32).T.astype(BF16)
         for i in range(2):
             wide_gain = jnp.broadcast_to(gain_ref[b, i : i + 1, :], (LANE, width)).T
             tgain[b, i] = jnp.concatenate([wide_gain] * TILES, 1)
-    for dy in range(3):
-        for dz in range(3):
-            cw[dy, dz * width : (dz + 1) * width, :] = jnp.concatenate(
-                [cw_ref[9 * dx + 3 * dy + dz].astype(F32) for dx in range(3)], 1
-            ).astype(BF16)
-
     win[...] = jnp.zeros_like(win)
+    loads[0].wait()
     wide[:, :sz, :] = vol_ref[...].reshape(sx * sy, sz, width).astype(F32)
 
     def gather(w, carry):
@@ -231,14 +237,24 @@
             1,
         )
 
-    for w in range(nwin):
-        for copy in copies1(w, False):
-            copy.wait()
-    for copy in copies1(0, True):
-        copy.wait()
-
     def second(i, carry):
         w = lax.rem(i + nwin - 1, nwin)
+
+        @pl.when(i == 0)
+        def _():
+            for copy in copies1(nwin - 1, False) + copies1(0, True):
+                copy.wait()
+
+        @pl.when(i == 1)
+        def _():
+            for copy in copies1(0, False):
+                copy.wait()
+
+        @pl.when((i > 0) & (i < nwin - 1))
+        def _():
+            for copy in copies1(i, False):
+                copy.wait()
+
         state = jnp.where(zlow == 1, natural1(w + 1), natural1(w))
         key_mask, query_mask = labels(w)
         out = block(state, key_mask, query_mask, *weights(1))
@@ -255,17 +271,18 @@
 
     lax.fori_loop(0, nwin, second, 0)
 
-    for w in range(nwin):
-        for copy in copies2(w, False):
-            copy.wait()
-    for copy in copies2(nwin - 1, True):
-        copy.wait()
+    loads[8].wait()
+    for dy in range(3):
+        for dz in range(3):
+            cw[dy, dz * width : (dz + 1) * width, :] = jnp.concatenate(
+                [cw_ref[9 * dx + 3 * dy + dz].astype(F32) for dx in range(3)], 1
+            ).astype(BF16)
 
     py = sy + 2
 
-    def spread(jj, carry):
-        high_at = lax.rem(jj, nwin + 1)
+    def spread(jj, partial):
         low_at = lax.rem(jj + nwin, nwin + 1)
+        high_at = jnp.where(partial, low_at, lax.rem(jj, nwin + 1))
         outer = jnp.where((jj == 0) | (jj == nwin + 1), 1, 0)
         above = jnp.where(here[2] < count[2] - 1, 1, 0)
         below = jnp.where(here[2] > 0, 1, 0)
@@ -300,39 +317,70 @@
                 if ok is not None:
                     value = jnp.where(ok, value, 0.0)
                 pad[(x + 1) * py + y + 1, pl.ds(1 + WINDOW * jj, WINDOW), :] = value
+
+    deep = cols.shape[1]
+
+    def convolve(chunk):
+        base = WINDOW + chunk * deep
+
+        def stack(xp, carry):
+            for y in range(py):
+                at = xp * py + y
+                cols[at] = jnp.concatenate(
+                    [pad[at, base + dz : base + dz + deep, :] for dz in range(3)], 1
+                ).astype(BF16)
+            total = None
+            for dy in range(3):
+                piece = cols[pl.ds(xp * py + dy, sy)].reshape(sy * deep, 3 * width)
+                part = dot(piece, cw[dy])
+                total = part if total is None else total + part
+            ys[xp] = total
+            return carry
+
+        lax.fori_loop(0, sx + 2, stack, 0)
+        size = min(deep, sz - chunk * deep)
+
+        def finish(x, carry):
+            total = (
+                ys[x][:, :width]
+                + ys[x + 1][:, width : 2 * width]
+                + ys[x + 2][:, 2 * width : 3 * width]
+            )
+            value = norm_rows(total, cg_ref[...])
+            value = jnp.where(value >= 0, value, 0.01 * value).reshape(sy, deep, width)
+            centre = pad[pl.ds((x + 1) * py + 1, sy), base + 1 : base + 1 + deep, :]
+            out_ref[x, :, chunk * deep : chunk * deep + size, :] = (centre + value)[
+                :, :size
+            ].astype(BF16)
+            return carry
+
+        lax.fori_loop(0, sx, finish, 0)
+
+    for w in range(nwin):
+        if w != nwin - 2:
+            for copy in copies2(w, False):
+                copy.wait()
+    for copy in copies2(nwin - 1, True):
+        copy.wait()
+
+    def spread_early(i, carry):
+        spread(lax.rem(i + nwin + 1, nwin + 2), i == nwin)
         return carry
 
-    lax.fori_loop(0, nwin + 2, spread, 0)
-
-    deep = cols.shape[1]
-
-    def stack(xp, carry):
-        for y in range(py):
-            at = xp * py + y
-            cols[at] = jnp.concatenate(
-                [pad[at, WINDOW + dz : WINDOW + dz + deep, :] for dz in range(3)], 1
-            ).astype(BF16)
-        total = None
-        for dy in range(3):
-            piece = cols[pl.ds(xp * py + dy, sy)].reshape(sy * deep, 3 * width)
-            part = dot(piece, cw[dy])
-            total = part if total is None else total + part
-        ys[xp] = total
+    def spread_late(i, carry):
+        spread(i, False)
         return carry
 
-    lax.fori_loop(0, sx + 2, stack, 0)
-
-    def finish(x, carry):
-        total = (
-            ys[x][:, :width] + ys[x + 1][:, width : 2 * width] + ys[x + 2][:, 2 * width : 3 * width]
-        )
-        value = norm_rows(total, cg_ref[...])
-        value = jnp.where(value >= 0, value, 0.01 * value).reshape(sy, deep, width)
-        centre = pad[pl.ds((x + 1) * py + 1, sy), WINDOW + 1 : WINDOW + 1 + deep, :]
-        out_ref[x] = (centre + value)[:, :sz].astype(BF16)
-        return carry
-
-    lax.fori_loop(0, sx, finish, 0)
+    lax.fori_loop(0, nwin + 1, spread_early, 0)
+    chunks = -(-sz // deep)
+    early = sum(deep * (c + 1) < WINDOW * (nwin - 2) + SHIFT for c in range(chunks))
+    for c in range(early):
+        convolve(c)
+    for copy in copies2(nwin - 2, False):
+        copy.wait()
+    lax.fori_loop(nwin - 1, nwin + 1, spread_late, 0)
+    for c in range(early, chunks):
+        convolve(c)
 
 
 def body(volume, w_qkv, w_proj, w_up, w_down, norm_gain, conv_weight, conv_gain):
@@ -346,12 +394,17 @@
     padded = (sx + 2) * (sy + 2)
     vmem = pl.BlockSpec(memory_space=pltpu.VMEM)
     sems = [pltpu.SemaphoreType.DMA((ncopy,))] * 4
+    operands = (
+        jnp.asarray(lane_facts()), volume, w_qkv, w_proj, w_up, jnp.swapaxes(w_down, 1, 2),
+        norm_gain, conv_weight, conv_gain.reshape(1, width),
+    )
     return pl.pallas_call(
         functools.partial(kernel, (sx, sy, sz, width)),
         out_shape=jax.ShapeDtypeStruct(volume.shape, BF16),
-        in_specs=[vmem] * 9,
+        in_specs=[pl.BlockSpec(memory_space=pltpu.HBM)] * 9,
         out_specs=vmem,
-        scratch_shapes=[
+        scratch_shapes=[pltpu.VMEM(o.shape, o.dtype) for o in operands]
+        + [
             pltpu.VMEM((sx * sy, deep, width), F32),
             pltpu.VMEM((nwin, LANES, width), F32),
             pltpu.VMEM((4, nwin + 1, TILES, width, LANE), BF16),
@@ -359,22 +412,19 @@
             pltpu.VMEM((2, 3 * width, width), BF16),
             pltpu.VMEM((2, width, width), BF16),
             pltpu.VMEM((2, hidden, width), BF16),
-            pltpu.VMEM((2, width, hidden), BF16),
             pltpu.VMEM((2, 2, width, LANES), F32),
             pltpu.VMEM((4, LANES, width), F32),
             pltpu.VMEM((padded, tall, width), F32),
-            pltpu.VMEM((padded, deep, 3 * width), BF16),
+            pltpu.VMEM((padded, 16, 3 * width), BF16),
             pltpu.VMEM((3, 3 * width, 3 * width), BF16),
-            pltpu.VMEM((sx + 2, sy * deep, 3 * width), F32),
+            pltpu.VMEM((sx + 2, sy * 16, 3 * width), F32),
         ]
-        + sems,
+        + sems
+        + [pltpu.SemaphoreType.DMA((9,))],
         compiler_params=pltpu.CompilerParams(
-            collective_id=0, has_side_effects=True, vmem_limit_bytes=48 * 1024 * 1024
+            collective_id=0, has_side_effects=True, vmem_limit_bytes=64 * 1024 * 1024 - 65536
         ),
-    )(
-        jnp.asarray(lane_facts()), volume, w_qkv, w_proj, w_up, w_down, norm_gain, conv_weight,
-        conv_gain.reshape(1, width),
-    )
+    )(*operands)
 
 
 def solution(mesh):

time: 39.8 us -> 38.4 us (0.965)
  local copies, waits for them, and re-layouts: 3.7 us -> 1.77 us
  Pallas kernels: 35.8 us -> 36.4 us
    unnamed x18 -> x1, local copies, waits for them, and re-layouts: 3.7 us -> 1.77 us
    pallas_call x1, Pallas kernels: 35.8 us -> 36.4 us  [body(): pl.pallas_call(functools.partial(kernel, (sx, sy, sz, width)), out_shape=...]
where the time goes in v2:
time: 38.4 us; the launch traced here: 38.2 us
  Pallas kernels  36.4 us (95%)
  local copies, waits for them, and re-layouts  1.77 us (5%)
    pallas_call x1, Pallas kernels, body(): pl.pallas_call(functools.partial(kernel, (sx, sy, sz, width)), out_shape=...  36.4 us
    unnamed x1, local copies, waits for them, and re-layouts  1.77 us

profile of v2, /device:TPU:0, one launch (start us, length us, event | category | flops | bytes accessed | tf_op | source)
XLA Modules:
  0.0 38.2 jit_solution(4889349024639756230)
XLA Ops:
  0.0 36.4 %shard_map.91 = bf16[7,7,28,48]{3,2,1,0:T(8,128)(2,1)} custom-call(s32[8,384]{1,0:T(8,128)} %constant.2.clone.facts_in, bf16[7,7,28,48]{3,2,1,0:T(8,128)(2,1)} %vol_in.1, bf16[2,48,144]{2,1,0:T(8,128)(2,1)} %wqkv_in.1, bf16[2,48,48]{2,1,0:T(8,128)(2,1)} %wproj_in.1, bf16[2,48,192]{2,1,0:T(8,128)(2,1)} %wup_in.1, bf16[2,48,192]{2,1,0:T(8,128)(2,1)} %bitcast.2, ...), custom_call_target="tpu_custom_call" | custom-call | tf_op jit(solution)/shard_map/pallas_call | solution.py:401
  36.4 1.8 %copy.11 = bf16[7,7,28,48]{3,2,1,0:T(8,128)(2,1)} copy(bf16[7,7,28,48]{3,2,1,0:T(8,128)(2,1)} %shard_map.91) | data formatting | bytes 263424

commit v3 on v2

--- a/solution.py
+++ b/solution.py
@@ -204,25 +204,27 @@
     plain_key, plain_query = masks(jnp.zeros((1, LANES), jnp.int32))
 
     def first(i, carry):
-        w = lax.rem(i + nwin - 1, nwin)
-        out = block(win[w].T, plain_key, plain_query, *weights(0))
-        put(r1, w, out)
+        pair = [lax.rem(2 * i + at + nwin - 1, nwin) for at in range(2)]
+        outs = [block(win[w].T, plain_key, plain_query, *weights(0)) for w in pair]
+        for w, out in zip(pair, outs):
+            put(r1, w, out)
 
         @pl.when(i == 0)
         def _():
             pl.semaphore_wait(barrier, 2 * len(others))
 
-        for copy in copies1(w, False):
-            copy.start()
-
-        @pl.when(w == 0)
+        for w in pair:
+            for copy in copies1(w, False):
+                copy.start()
+
+        @pl.when(i == 0)
         def _():
             for copy in copies1(0, True):
                 copy.start()
 
         return carry
 
-    lax.fori_loop(0, nwin, first, 0)
+    lax.fori_loop(0, nwin // 2, first, 0)
 
     def natural1(j):
         both = (xlow * ylow) == 1
@@ -385,7 +387,7 @@
 
 def body(volume, w_qkv, w_proj, w_up, w_down, norm_gain, conv_weight, conv_gain):
     sx, sy, sz, width = volume.shape
-    assert sx == WINDOW and sy == WINDOW and sz % WINDOW == 0
+    assert sx == WINDOW and sy == WINDOW and sz % (2 * WINDOW) == 0
     nwin = sz // WINDOW
     hidden = w_up.shape[-1]
     deep = -(-sz // 16) * 16

time: 38.4 us -> 37.7 us (0.982)
  Pallas kernels: 36.4 us -> 35.7 us
    pallas_call x1, Pallas kernels: 36.4 us -> 35.7 us  [body(): pl.pallas_call(functools.partial(kernel, (sx, sy, sz, width)), out_shape=...]
where the time goes in v3:
time: 37.7 us; the launch traced here: 37.5 us
  Pallas kernels  35.7 us (95%)
  local copies, waits for them, and re-layouts  1.77 us (5%)
    pallas_call x1, Pallas kernels, body(): pl.pallas_call(functools.partial(kernel, (sx, sy, sz, width)), out_shape=...  35.7 us
    unnamed x1, local copies, waits for them, and re-layouts  1.77 us

profile of v3, /device:TPU:0, one launch (start us, length us, event | category | flops | bytes accessed | tf_op | source)
XLA Modules:
  0.0 37.5 jit_solution(17210120652694436022)
XLA Ops:
  0.0 35.7 %shard_map.91 = bf16[7,7,28,48]{3,2,1,0:T(8,128)(2,1)} custom-call(s32[8,384]{1,0:T(8,128)} %constant.2.clone.facts_in, bf16[7,7,28,48]{3,2,1,0:T(8,128)(2,1)} %vol_in.1, bf16[2,48,144]{2,1,0:T(8,128)(2,1)} %wqkv_in.1, bf16[2,48,48]{2,1,0:T(8,128)(2,1)} %wproj_in.1, bf16[2,48,192]{2,1,0:T(8,128)(2,1)} %wup_in.1, bf16[2,48,192]{2,1,0:T(8,128)(2,1)} %bitcast.2, ...), custom_call_target="tpu_custom_call" | custom-call | tf_op jit(solution)/shard_map/pallas_call | solution.py:403
  35.7 1.8 %copy.11 = bf16[7,7,28,48]{3,2,1,0:T(8,128)(2,1)} copy(bf16[7,7,28,48]{3,2,1,0:T(8,128)(2,1)} %shard_map.91) | data formatting | bytes 263424

commit v4 on v3

--- a/solution.py
+++ b/solution.py
@@ -339,7 +339,7 @@
             ys[xp] = total
             return carry
 
-        lax.fori_loop(0, sx + 2, stack, 0)
+        lax.fori_loop(0, sx + 2, stack, 0, unroll=3)
         size = min(deep, sz - chunk * deep)
 
         def finish(x, carry):
@@ -356,7 +356,7 @@
             ].astype(BF16)
             return carry
 
-        lax.fori_loop(0, sx, finish, 0)
+        lax.fori_loop(0, sx, finish, 0, unroll=True)
 
     for w in range(nwin):
         if w != nwin - 2:

time: 37.7 us -> 33.6 us (0.89)
  Pallas kernels: 35.7 us -> 31.7 us
    pallas_call x1, Pallas kernels: 35.7 us -> 31.7 us  [body(): pl.pallas_call(functools.partial(kernel, (sx, sy, sz, width)), out_shape=...]
where the time goes in v4:
time: 33.6 us; the launch traced here: 33.5 us
  Pallas kernels  31.7 us (94%)
  local copies, waits for them, and re-layouts  1.77 us (5%)
    pallas_call x1, Pallas kernels, body(): pl.pallas_call(functools.partial(kernel, (sx, sy, sz, width)), out_shape=...  31.7 us
    unnamed x1, local copies, waits for them, and re-layouts  1.77 us

profile of v4, /device:TPU:0, one launch (start us, length us, event | category | flops | bytes accessed | tf_op | source)
XLA Modules:
  0.0 33.5 jit_solution(13088926964203285968)
XLA Ops:
  0.0 31.7 %shard_map.91 = bf16[7,7,28,48]{3,2,1,0:T(8,128)(2,1)} custom-call(s32[8,384]{1,0:T(8,128)} %constant.2.clone.facts_in, bf16[7,7,28,48]{3,2,1,0:T(8,128)(2,1)} %vol_in.1, bf16[2,48,144]{2,1,0:T(8,128)(2,1)} %wqkv_in.1, bf16[2,48,48]{2,1,0:T(8,128)(2,1)} %wproj_in.1, bf16[2,48,192]{2,1,0:T(8,128)(2,1)} %wup_in.1, bf16[2,48,192]{2,1,0:T(8,128)(2,1)} %bitcast.2, ...), custom_call_target="tpu_custom_call" | custom-call | tf_op jit(solution)/shard_map/pallas_call | solution.py:403
  31.7 1.8 %copy.11 = bf16[7,7,28,48]{3,2,1,0:T(8,128)(2,1)} copy(bf16[7,7,28,48]{3,2,1,0:T(8,128)(2,1)} %shard_map.91) | data formatting | bytes 263424

commit v5 on v4

--- a/solution.py
+++ b/solution.py
@@ -339,7 +339,7 @@
             ys[xp] = total
             return carry
 
-        lax.fori_loop(0, sx + 2, stack, 0, unroll=3)
+        lax.fori_loop(0, sx + 2, stack, 0, unroll=True)
         size = min(deep, sz - chunk * deep)
 
         def finish(x, carry):

time: 33.6 us -> 31.8 us (0.946)
  Pallas kernels: 31.7 us -> 29.9 us
    pallas_call x1, Pallas kernels: 31.7 us -> 29.9 us  [body(): pl.pallas_call(functools.partial(kernel, (sx, sy, sz, width)), out_shape=...]
where the time goes in v5:
time: 31.8 us; the launch traced here: 31.7 us
  Pallas kernels  29.9 us (94%)
  local copies, waits for them, and re-layouts  1.77 us (6%)
    pallas_call x1, Pallas kernels, body(): pl.pallas_call(functools.partial(kernel, (sx, sy, sz, width)), out_shape=...  29.9 us
    unnamed x1, local copies, waits for them, and re-layouts  1.77 us

profile of v5, /device:TPU:0, one launch (start us, length us, event | category | flops | bytes accessed | tf_op | source)
XLA Modules:
  0.0 31.7 jit_solution(4875103332059112445)
XLA Ops:
  0.0 29.9 %shard_map.91 = bf16[7,7,28,48]{3,2,1,0:T(8,128)(2,1)} custom-call(s32[8,384]{1,0:T(8,128)} %constant.2.clone.facts_in, bf16[7,7,28,48]{3,2,1,0:T(8,128)(2,1)} %vol_in.1, bf16[2,48,144]{2,1,0:T(8,128)(2,1)} %wqkv_in.1, bf16[2,48,48]{2,1,0:T(8,128)(2,1)} %wproj_in.1, bf16[2,48,192]{2,1,0:T(8,128)(2,1)} %wup_in.1, bf16[2,48,192]{2,1,0:T(8,128)(2,1)} %bitcast.2, ...), custom_call_target="tpu_custom_call" | custom-call | tf_op jit(solution)/shard_map/pallas_call | solution.py:403
  29.9 1.8 %copy.11 = bf16[7,7,28,48]{3,2,1,0:T(8,128)(2,1)} copy(bf16[7,7,28,48]{3,2,1,0:T(8,128)(2,1)} %shard_map.91) | data formatting | bytes 263424
